TPU v7x, 512 devices: a whole 4x8x8 slice. The times are simulated.
512 devices in a mesh: dp: 2 (over x_hi), ffn: 16 (over z, core), hid: 16 (over y, x_lo).
Axes of the slice: x: 4 (x_hi: 2, x_lo: 2; x = x_hi * 2 + x_lo), y: 8, z: 8, core: 2. Of those that a mesh axis runs over, the one named last changes fastest.
Arguments:
- stream: bfloat16 [512, 16384], P('dp', 'hid'), may hold values from -160 to 160
- steering: float32 [16384], P('hid'), may hold values from -40 to 40
- strength: float32 [512], P('dp'), may hold values from 0.5 to 2
- norm_gain_vector: float32 [16384], P('hid'), may hold values from 0.25 to 1.75
- frozen_weights: bfloat16 [2, 16384, 26624], P('dp', 'hid', 'ffn'), may hold values from -0.046875 to 0.046875
- adapter_down_factors: bfloat16 [2, 16384, 16], P(None, 'hid'), may hold values from -0.046875 to 0.046875
- adapter_up_factors: bfloat16 [2, 16, 26624], P(None, None, 'ffn'), may hold values from -1.5 to 1.5
- cotangent: bfloat16 [512, 26624], P(('dp', 'hid'), 'ffn'), may hold values from -6 to 6
Outputs:
- residual_stream_gradient: bfloat16 [512, 16384], P('dp', 'hid')
- steering_vector_gradient: float32 [16384], P('hid')
- adapter_down_gradient: float32 [2, 16384, 16], P(None, 'hid')
- adapter_up_gradient: float32 [2, 16, 26624], P(None, None, 'ffn')
All inputs are finite; a program needn't handle non-finite values.
Results may differ from a plain program's by a relative error of at most 0.0068.
Values may be sent and summed in bfloat16 or wider, within the bound.
A program may use at most 64 MiB of HBM per device.

v0:
```python
import jax
import jax.numpy as jnp
from jax import lax
from jax.sharding import PartitionSpec as P

MODEL_WIDTH = 16384
ADAPTER_SCALE = 0.5


def gated_layer_backward(
    preactivation_values, adapter_input_rows, adapter_up_factors, incoming_gradient
):
    activation_values = preactivation_values + ADAPTER_SCALE * jnp.einsum(
        "dch,chn->dcn", adapter_input_rows, adapter_up_factors, preferred_element_type=jnp.float32
    )
    gate_values = activation_values[:, 0]
    up_projection_values = activation_values[:, 1]
    sigma = jax.nn.sigmoid(gate_values)
    flow = incoming_gradient.astype(jnp.float32)
    gate_grad = flow * up_projection_values * sigma * (1.0 + gate_values * (1.0 - sigma))
    upper_grad = flow * gate_values * sigma
    return jnp.stack([gate_grad, upper_grad], axis=1).astype(jnp.bfloat16)


def local(
    stream,
    steering,
    strength,
    norm_gain_vector,
    frozen_weights,
    adapter_down_factors,
    adapter_up_factors,
    cotangent,
):
    rows = stream.astype(jnp.float32)
    row_squares = jnp.sum(rows * rows, axis=1)
    steer_power = jnp.sum(steering * steering)
    total_rows, total_steer = lax.psum((row_squares, steer_power), "hid")
    stream_ms = total_rows / MODEL_WIDTH + 1e-06
    steer_ms = total_steer / MODEL_WIDTH + 1e-06
    scale = strength * jnp.sqrt(stream_ms / steer_ms)
    steered = rows + scale[:, None] * steering[None, :]
    steered_power = lax.psum(jnp.sum(steered * steered, axis=1), "hid")
    inv_rms = lax.rsqrt(steered_power / MODEL_WIDTH + 1e-05)
    normalized_input = (steered * inv_rms[:, None] * norm_gain_vector[None, :]).astype(jnp.bfloat16)
    down_piece = jnp.einsum(
        "jq,hqp->jhp", normalized_input, adapter_down_factors, preferred_element_type=jnp.float32
    )
    weights = lax.all_gather(frozen_weights, "dp", axis=0, tiled=True)
    full_acts = jnp.einsum(
        "td,kdf->tkf", normalized_input, weights, preferred_element_type=jnp.float32
    )
    preactivation_values, adapter_sum = lax.psum((full_acts, down_piece), "hid")
    incoming_gradient = lax.all_gather(cotangent, "hid", axis=0, tiled=True)
    adapter_input_rows = adapter_sum.astype(jnp.bfloat16)
    activation_gradient = gated_layer_backward(
        preactivation_values, adapter_input_rows, adapter_up_factors, incoming_gradient
    )
    grad_share = lax.psum_scatter(
        jnp.einsum("tkf,kdf->td", activation_gradient, weights, preferred_element_type=jnp.float32),
        "ffn",
        scatter_dimension=0,
        tiled=True,
    )
    input_frozen_term = lax.all_gather(grad_share, "ffn", axis=0, tiled=True)
    backward_piece = jnp.einsum(
        "sua,uqa->suq", activation_gradient, adapter_up_factors, preferred_element_type=jnp.float32
    )
    back_sum = lax.psum(backward_piece, "ffn")
    lowrank_backward = back_sum.astype(jnp.bfloat16)
    normalized_gradient = input_frozen_term + ADAPTER_SCALE * jnp.einsum(
        "qme,mfe->qf", lowrank_backward, adapter_down_factors, preferred_element_type=jnp.float32
    )
    product = (
        lax.psum(jnp.sum(steered * norm_gain_vector[None, :] * normalized_gradient, axis=1), "hid")
        / MODEL_WIDTH
    )
    steered_grad = (
        inv_rms[:, None] * norm_gain_vector[None, :] * normalized_gradient
        - (inv_rms**3 * product)[:, None] * steered
    )
    residual_stream_gradient = steered_grad.astype(jnp.bfloat16)
    steering_part = jnp.sum(scale[:, None] * steered_grad, axis=0)
    down_projection_gradient = ADAPTER_SCALE * jnp.einsum(
        "cl,can->aln", normalized_input, lowrank_backward, preferred_element_type=jnp.float32
    )
    up_projection_gradient = ADAPTER_SCALE * jnp.einsum(
        "qyj,qyi->yji", adapter_input_rows, activation_gradient, preferred_element_type=jnp.float32
    )
    down_projection_gradient, up_projection_gradient, steering_vector_gradient = lax.psum(
        (down_projection_gradient, up_projection_gradient, steering_part), "dp"
    )
    return (
        residual_stream_gradient,
        steering_vector_gradient,
        down_projection_gradient,
        up_projection_gradient,
    )


def solution(mesh):
    in_specs = (
        P("dp", "hid"),
        P("hid"),
        P("dp"),
        P("hid"),
        P("dp", "hid", "ffn"),
        P(None, "hid", None),
        P(None, None, "ffn"),
        P(("dp", "hid"), "ffn"),
    )
    out_specs = (P("dp", "hid"), P("hid"), P(None, "hid", None), P(None, None, "ffn"))
    return jax.shard_map(local, mesh=mesh, in_specs=in_specs, out_specs=out_specs, check_vma=False)
```

profile of v0, /device:TPU:1, one launch (start us, length us, event | category | flops | bytes accessed | tf_op | source)
XLA Modules:
  0.0 484.7 jit_solution(4777915458065586716)
XLA Ops:
  7.2 0.0 copy-start
  7.2 0.0 copy-start.5
  7.2 0.0 copy-start.1
  7.2 0.0 copy-start.8
  7.2 0.0 copy-start.7
  7.2 0.0 all-gather.3.cloned.1.call-start
  7.3 0.7 all-gather.3.cloned.1.call-update
  8.0 0.0 all-reduce.5.cloned.1.call-start
  8.0 0.0 copy-done.5
  8.0 0.6 multiply_reduce_fusion.3
  8.6 0.0 copy-done.1
  8.6 0.2 fusion.8
  8.8 29.3 %all-reduce = (f32[256]{0:T(256)S(1)}, f32[]{:T(128)}) all-reduce(f32[256]{0:T(256)S(1)} %fusion.8, f32[]{:T(128)} %multiply_reduce_fusion.3), channel_id=1, replica_groups=mesh['dp'=2,'ffn'=16,'hid'=16] {'hid'}, use_global_device_ids=true, to_apply=%region_1.0 | all-reduce | flops 257 | bytes 2056 | tf_op jit(solution)/shard_map/psum | solution.py:38
  38.8 0.0 copy-done.8
  38.8 0.3 multiply_reduce_fusion.2
  39.1 25.7 %psum.72 = f32[256]{0:T(256)S(1)} all-reduce(f32[256]{0:T(256)S(1)} %multiply_reduce_fusion.2), channel_id=1, replica_groups=mesh['dp'=2,'ffn'=16,'hid'=16] {'hid'}, use_global_device_ids=true, to_apply=%region_5.0 | all-reduce | flops 256 | bytes 2048 | tf_op jit(solution)/shard_map/psum | solution.py:43
  64.9 0.0 copy-done.7
  64.9 0.3 multiply_convert_fusion
  65.1 47.6 %all-gather.3.cloned.1.call-done = bf16[2,1024,1664]{2,1,0:T(8,128)(2,1)} async-done(((bf16[1,1024,1664]{2,1,0:T(8,128)(2,1)}), bf16[2,1024,1664]{2,1,0:T(8,128)(2,1)}) %all-gather.3.cloned.1.call-update) | async-done | bytes 6815760 | tf_op jit(solution)/shard_map/all_gather | solution.py:49
  112.8 6.7 %fusion.12 = f32[256,2,1664]{2,0,1:T(8,128)} fusion(bf16[2,1024,1664]{2,1,0:T(8,128)(2,1)} %all-gather.3.cloned.1.call-done, bf16[256,1024]{1,0:T(8,128)(2,1)S(1)} %multiply_convert_fusion), kind=kOutput, calls=%fused_computation.31 | convolution fusion | flops 1744830464 | bytes 10747904 | tf_op jit(solution)/shard_map/td,kdf->tkf/dot_general | solution.py:50
  119.5 0.0 copy-start.4
  119.5 0.0 copy-start.6
  119.5 0.0 all-reduce.5.cloned.1.call-update
  119.5 0.0 reduce-scatter.2.cloned.1.call-start
  119.6 0.8 copy-done.4
  120.3 0.2 fusion.22
  120.6 50.2 %psum.74 = bf16[256,2,16]{0,2,1:T(8,128)(2,1)S(1)} all-reduce(f32[256,2,16]{0,2,1:T(8,128)S(1)} %bitcast.55), channel_id=1, replica_groups=mesh['dp'=2,'ffn'=16,'hid'=16] {'hid'}, use_global_device_ids=true, to_apply=%region_7.0 | all-reduce | flops 8192 | bytes 49152 | tf_op jit(solution)/shard_map/psum | solution.py:53
  170.8 0.0 copy-done.6
  170.8 53.1 %all_gather.9 = bf16[256,1664]{1,0:T(8,128)(2,1)S(1)} all-gather(bf16[16,1664]{1,0:T(8,128)(2,1)S(1)} %copy-done.6), channel_id=1, replica_groups=mesh['dp'=2,'ffn'=16,'hid'=16] {'hid'}, dimensions={0}, use_global_device_ids=true | all-gather | bytes 905216 | tf_op jit(solution)/shard_map/all_gather | solution.py:54
  223.9 82.8 %all-reduce.5.cloned.1.call-done = f32[256,2,1664]{2,0,1:T(8,128)} async-done(((f32[256,2,1664]{2,0,1:T(8,128)}), f32[256,2,1664]{2,0,1:T(8,128)}) %all-reduce.5.cloned.1.call-update) | async-done | bytes 3407888 | tf_op jit(solution)/shard_map/psum | solution.py:53
  306.7 0.0 copy-done
  306.7 2.6 bitcast_add_fusion
  309.3 0.9 fusion.10
  310.2 0.0 copy-start.2
  310.2 1.0 copy-done.2
  311.2 5.9 %convolution_bitcast_fusion.1 = f32[256,1024]{1,0:T(8,128)} fusion(bf16[2,1024,1664]{2,1,0:T(8,128)(2,1)} %all-gather.3.cloned.1.call-done, bf16[256,1,1664]{2,0,1:T(8,128)(2,1)S(1)} %get-tuple-element.11, bf16[256,1,1664]{2,0,1:T(8,128)(2,1)S(1)} %get-tuple-element.10), kind=kOutput, calls=%fused_computation.16 | convolution fusion | flops 1745682432 | bytes 9568256 | tf_op jit(solution)/shard_map/tkf,kdf->td/dot_general | solution.py:60
  317.0 0.0 reduce-scatter.2.cloned.1.call-update
  317.1 0.0 copy-start.3
  317.1 0.0 all-gather.5.cloned.1.call-start
  317.1 60.2 %reduce-scatter.2.cloned.1.call-done = f32[16,1024]{1,0:T(8,128)} async-done(((f32[256,1024]{1,0:T(8,128)}), f32[16,1024]{1,0:T(8,128)}) %reduce-scatter.2.cloned.1.call-update) | async-done | bytes 65552 | tf_op jit(solution)/shard_map/reduce_scatter | solution.py:59
  377.3 0.0 all-gather.5.cloned.1.call-update
  377.3 0.0 all-reduce.7.cloned.1.call-start
  377.4 1.7 convolution_bitcast_fusion.2
  379.1 46.5 %psum.75 = bf16[256,2,16]{0,2,1:T(8,128)(2,1)S(1)} all-reduce(f32[256,2,16]{0,2,1:T(8,128)S(1)} %convolution_bitcast_fusion.2), channel_id=1, replica_groups=mesh['dp'=2,'ffn'=16,'hid'=16] {'ffn'}, use_global_device_ids=true, to_apply=%region_9.0 | all-reduce | flops 8192 | bytes 49152 | tf_op jit(solution)/shard_map/psum | solution.py:69
  425.6 0.0 copy-done.3
  425.6 1.1 convolution_multiply_fusion
  426.6 0.9 fusion.7
  427.5 0.0 all-reduce.7.cloned.1.call-update
  427.5 0.0 all-gather.5.cloned.1.call-done
  427.6 1.7 multiply_reduce_fusion.1
  429.3 27.7 %psum.76 = f32[256]{0:T(256)S(1)} all-reduce(f32[256]{0:T(256)S(1)} %get-tuple-element.12), channel_id=1, replica_groups=mesh['dp'=2,'ffn'=16,'hid'=16] {'hid'}, use_global_device_ids=true, to_apply=%region_11.0 | all-reduce | flops 256 | bytes 2048 | tf_op jit(solution)/shard_map/psum | solution.py:75
  457.0 1.2 multiply_reduce_fusion
  458.2 5.9 %psum.77 = f32[1024]{0:T(1024)} all-reduce(f32[1024]{0:T(1024)S(1)} %get-tuple-element.8), channel_id=1, replica_groups=mesh['dp'=2,'ffn'=16,'hid'=16] {'dp'}, use_global_device_ids=true, to_apply=%region_13.0 | all-reduce | flops 1024 | bytes 8192 | tf_op jit(solution)/shard_map/psum | solution.py:90
  464.1 10.9 %all-reduce.7.cloned.1.call-done = (f32[2,1024,16]{1,2,0:T(8,128)}, f32[2,16,1664]{2,1,0:T(8,128)}) async-done(((f32[2,1024,16]{1,2,0:T(8,128)}, f32[2,16,1664]{2,1,0:T(8,128)}), (f32[2,1024,16]{1,2,0:T(8,128)}, f32[2,16,1664]{2,1,0:T(8,128)})) %all-reduce.7.cloned.1.call-update) | async-done | bytes 344080 | tf_op jit(solution)/shard_map/psum | solution.py:90
  475.0 1.6 copy.15
  476.5 1.6 copy.16
  (3 shorter events, 0.0 us)
Async XLA Ops:
  7.2 299.6 %copy-start = (bf16[2,16,1664]{2,1,0:T(8,128)(2,1)S(1)}, bf16[2,16,1664]{2,1,0:T(8,128)(2,1)}, u32[]{:S(2)}) copy-start(bf16[2,16,1664]{2,1,0:T(8,128)(2,1)} %param.14) | copy-start | bytes 319492
  7.2 0.8 copy-start.5
  7.2 1.4 copy-start.1
  7.2 31.6 %copy-start.8 = (f32[256]{0:T(256)S(1)}, f32[256]{0:T(256)}, u32[]{:S(2)}) copy-start(f32[256]{0:T(256)} %param.10) | copy-start | bytes 3076
  7.2 57.6 %copy-start.7 = (f32[1024]{0:T(1024)S(1)}, f32[1024]{0:T(1024)}, u32[]{:S(2)}) copy-start(f32[1024]{0:T(1024)} %param.11) | copy-start | bytes 12292
  7.2 105.6 %all-gather.3.cloned.1.call-start = ((), (), s32[]{:S(2)}) async-start(), calls=%async_computation.1 | async-start | bytes 10223616 | tf_op jit(solution)/shard_map/all_gather | solution.py:49
  8.0 298.8 %all-reduce.5.cloned.1.call-start = ((), (), s32[]{:S(2)}) async-start(), calls=%async_computation.2 | async-start | bytes 6815744 | tf_op jit(solution)/shard_map/psum | solution.py:53
  119.5 0.8 copy-start.4
  119.5 51.3 %copy-start.6 = (bf16[16,1664]{1,0:T(8,128)(2,1)S(1)}, bf16[16,1664]{1,0:T(8,128)(2,1)}, u32[]{:S(2)}) copy-start(bf16[16,1664]{1,0:T(8,128)(2,1)} %param.15) | copy-start | bytes 159748
  119.5 257.8 %reduce-scatter.2.cloned.1.call-start = ((), (), s32[]{:S(2)}) async-start(), calls=%async_computation.3 | async-start | bytes 1114112 | tf_op jit(solution)/shard_map/reduce_scatter | solution.py:59
  310.2 1.0 copy-start.2
  317.1 108.5 %copy-start.3 = (bf16[256,1,1664]{2,0,1:T(8,128)(2,1)S(1)}, bf16[256,1,1664]{2,0,1:T(8,128)(2,1)}, u32[]{:S(2)}) copy-start(bf16[256,1,1664]{2,0,1:T(8,128)(2,1)} %copy-done.2) | copy-start | bytes 2555908
  317.1 110.5 %all-gather.5.cloned.1.call-start = ((), (), s32[]{:S(2)}) async-start(), calls=%async_computation.4 | async-start | bytes 1114112 | tf_op jit(solution)/shard_map/all_gather | solution.py:65
  377.3 97.7 %all-reduce.7.cloned.1.call-start = ((), (), s32[]{:S(2)}) async-start(), calls=%async_computation.5 | async-start | bytes 688128 | tf_op jit(solution)/shard_map/psum | solution.py:90
Sparse Core Ops, SparseCore 0:
  10.1 102.5 all-gather.2
  119.6 187.0 all-reduce.4
  317.2 60.0 reduce-scatter.1
  379.3 43.0 all-gather.4
  427.7 47.2 all-reduce.6
where the time goes:
time: 485 us
  blocking collectives  238 us (49%)
  waiting for transfers between devices  202 us (42%)
  matrix products  20.7 us (4%)
  between operations  14.6 us (3%)
  local copies, waits for them, and re-layouts  4.97 us (1%)
    psum x1, waiting for transfers between devices, local(): preactivation_values, adapter_sum = lax.psum((full_acts, down_piece), 'hid')  82.8 us
    reduce_scatter x1, waiting for transfers between devices, local(): lax.psum_scatter(jnp.einsum('tkf,kdf->td', activation_gradient, weights,...  60.2 us
    all_gather x1, blocking collectives, local(): incoming_gradient = lax.all_gather(cotangent, 'hid', axis=0, tiled=True)  53.1 us
    psum x1, blocking collectives, local(): preactivation_values, adapter_sum = lax.psum((full_acts, down_piece), 'hid')  50.2 us
    all_gather x1, waiting for transfers between devices, local(): weights = lax.all_gather(frozen_weights, 'dp', axis=0, tiled=True)  47.6 us
    psum x1, blocking collectives, local(): back_sum = lax.psum(backward_piece, 'ffn')  46.5 us
    psum x1, blocking collectives, local(): total_rows, total_steer = lax.psum((row_squares, steer_power), 'hid')  29.3 us
    psum x1, blocking collectives, local(): lax.psum(jnp.sum(steered * norm_gain_vector[None, :] * normalized_gradien...  27.7 us
  transfers between devices with their start and end apart: 5, of which 4 were waited for; matrix products, arithmetic and copies ran while one was open for 2% of the time, Pallas kernels for 0%

commit v1 on v0

--- a/solution.py
+++ b/solution.py
@@ -46,7 +46,8 @@
     down_piece = jnp.einsum(
         "jq,hqp->jhp", normalized_input, adapter_down_factors, preferred_element_type=jnp.float32
     )
-    weights = lax.all_gather(frozen_weights, "dp", axis=0, tiled=True)
+    outgoing = jnp.stack([frozen_weights] * lax.axis_size("dp"))
+    weights = jnp.concatenate(lax.all_to_all(outgoing, "dp", 0, 0), axis=0)
     full_acts = jnp.einsum(
         "td,kdf->tkf", normalized_input, weights, preferred_element_type=jnp.float32
     )

time: 485 us -> 535 us (1.10)
  blocking collectives: 238 us -> 301 us
  waiting for transfers between devices: 202 us -> 177 us
  starting transfers between devices: 0.2 us -> 6.75 us
  other arithmetic: 3.47 us -> 10 us
    psum x1, blocking collectives: 29.3 us -> 96.6 us  [local(): total_rows, total_steer = lax.psum((row_squares, steer_power), 'hid')]
    all_gather x1 -> x0, waiting for transfers between devices: 47.6 us -> none  [local(): weights = lax.all_gather(frozen_weights, 'dp', axis=0, tiled=True)]
    psum x1, waiting for transfers between devices: 82.8 us -> 105 us  [local(): preactivation_values, adapter_sum = lax.psum((full_acts, down_piece), 'hid')]
    all_to_all x0 -> x1, starting transfers between devices: none -> 6.59 us  [local(): weights = jnp.concatenate(lax.all_to_all(outgoing, 'dp', 0, 0), axis=0)]
    another operation x0 -> x1, other arithmetic: none -> 6.56 us  [local(): outgoing = jnp.stack([frozen_weights] * lax.axis_size('dp'))]
  transfers between devices with their start and end apart: 5 -> 5, of which waited for: 4 -> 3; matrix products, arithmetic and copies ran while one was open for 2% -> 2% of each run, Pallas kernels for 0% -> 0%
where the time goes in v1:
time: 535 us
  blocking collectives  301 us (56%)
  waiting for transfers between devices  177 us (33%)
  matrix products  20.7 us (4%)
  between operations  14.5 us (3%)
  other arithmetic  10 us (2%)
  starting transfers between devices  6.75 us (1%)
    psum x1, waiting for transfers between devices, local(): preactivation_values, adapter_sum = lax.psum((full_acts, down_piece), 'hid')  105 us
    psum x1, blocking collectives, local(): total_rows, total_steer = lax.psum((row_squares, steer_power), 'hid')  96.6 us
    reduce_scatter x1, waiting for transfers between devices, local(): lax.psum_scatter(jnp.einsum('tkf,kdf->td', activation_gradient, weights,...  60.1 us
    all_gather x1, blocking collectives, local(): incoming_gradient = lax.all_gather(cotangent, 'hid', axis=0, tiled=True)  51.5 us
    psum x1, blocking collectives, local(): preactivation_values, adapter_sum = lax.psum((full_acts, down_piece), 'hid')  49.3 us
    psum x1, blocking collectives, local(): back_sum = lax.psum(backward_piece, 'ffn')  46.8 us
    psum x1, blocking collectives, local(): lax.psum(jnp.sum(steered * norm_gain_vector[None, :] * normalized_gradien...  27.5 us
    psum x1, blocking collectives, local(): steered_power = lax.psum(jnp.sum(steered * steered, axis=1), 'hid')  23.7 us
  transfers between devices with their start and end apart: 5, of which 3 were waited for; matrix products, arithmetic and copies ran while one was open for 2% of the time, Pallas kernels for 0%

profile of v1, /device:TPU:1, one launch (start us, length us, event | category | flops | bytes accessed | tf_op | source)
XLA Modules:
  0.0 534.8 jit_solution(4729848772424664306)
XLA Ops:
  7.2 0.0 copy-start
  7.2 6.6 %pad_maximum_fusion = bf16[2,1,1024,1664]{3,2,1,0:T(8,128)(2,1)} fusion(bf16[1,1,1024,1664]{3,2,1,0:T(8,128)(2,1)} %bitcast.60), kind=kLoop, calls=%fused_computation | loop fusion | flops 3407872 | bytes 10223616 | tf_op jit(solution)/shard_map/stack | solution.py:49
  13.7 0.0 copy-start.5
  13.7 0.0 copy-start.1
  13.7 0.0 copy-start.8
  13.7 0.0 copy-start.7
  13.8 6.6 %all-to-all-start = ((bf16[2,1,1024,1664]{3,2,1,0:T(8,128)(2,1)}), bf16[2,1,1024,1664]{3,2,1,0:T(8,128)(2,1)}, u32[]{:S(2)}, u32[]{:S(2)}) async-start(bf16[2,1,1024,1664]{3,2,1,0:T(8,128)(2,1)} %pad_maximum_fusion), calls=%async_computation | async-start | bytes 13631488 | tf_op jit(solution)/shard_map/all_to_all | solution.py:50
  20.3 0.0 all-reduce.5.cloned.1.call-start
  20.4 0.0 copy-done.5
  20.4 0.6 multiply_reduce_fusion.3
  21.0 0.0 copy-done.1
  21.0 0.2 fusion.15
  21.2 96.6 %all-reduce = (f32[256]{0:T(256)S(1)}, f32[]{:T(128)}) all-reduce(f32[256]{0:T(256)S(1)} %fusion.15, f32[]{:T(128)} %multiply_reduce_fusion.3), channel_id=1, replica_groups=mesh['dp'=2,'ffn'=16,'hid'=16] {'hid'}, use_global_device_ids=true, to_apply=%region_1.0 | all-reduce | flops 257 | bytes 2056 | tf_op jit(solution)/shard_map/psum | solution.py:38
  118.4 0.0 copy-done.8
  118.4 0.3 multiply_reduce_fusion.2
  118.8 23.7 %psum.72 = f32[256]{0:T(256)S(1)} all-reduce(f32[256]{0:T(256)S(1)} %multiply_reduce_fusion.2), channel_id=1, replica_groups=mesh['dp'=2,'ffn'=16,'hid'=16] {'hid'}, use_global_device_ids=true, to_apply=%region_5.0 | all-reduce | flops 256 | bytes 2048 | tf_op jit(solution)/shard_map/psum | solution.py:43
  142.4 0.0 copy-done.7
  142.4 0.3 multiply_convert_fusion
  142.7 0.0 all-to-all-done
  142.7 6.7 %fusion.2 = f32[256,2,1664]{2,0,1:T(8,128)} fusion(bf16[2,1,1024,1664]{3,2,1,0:T(8,128)(2,1)} %all-to-all-done, bf16[256,1024]{1,0:T(8,128)(2,1)S(1)} %multiply_convert_fusion), kind=kOutput, calls=%fused_computation.3 | convolution fusion | flops 1744830464 | bytes 10747904 | tf_op jit(solution)/shard_map/td,kdf->tkf/dot_general | solution.py:51
  149.4 0.0 copy-start.4
  149.4 0.0 copy-start.6
  149.4 0.0 all-reduce.5.cloned.1.call-update
  149.5 0.0 reduce-scatter.2.cloned.1.call-start
  149.5 0.8 copy-done.4
  150.3 0.2 fusion.28
  150.5 49.3 %psum.74 = bf16[256,2,16]{0,2,1:T(8,128)(2,1)S(1)} all-reduce(f32[256,2,16]{0,2,1:T(8,128)S(1)} %bitcast.62), channel_id=1, replica_groups=mesh['dp'=2,'ffn'=16,'hid'=16] {'hid'}, use_global_device_ids=true, to_apply=%region_7.0 | all-reduce | flops 8192 | bytes 49152 | tf_op jit(solution)/shard_map/psum | solution.py:54
  199.8 0.0 copy-done.6
  199.8 51.5 %all_gather.6 = bf16[256,1664]{1,0:T(8,128)(2,1)S(1)} all-gather(bf16[16,1664]{1,0:T(8,128)(2,1)S(1)} %copy-done.6), channel_id=1, replica_groups=mesh['dp'=2,'ffn'=16,'hid'=16] {'hid'}, dimensions={0}, use_global_device_ids=true | all-gather | bytes 905216 | tf_op jit(solution)/shard_map/all_gather | solution.py:55
  251.3 105.3 %all-reduce.5.cloned.1.call-done = f32[256,2,1664]{2,0,1:T(8,128)} async-done(((f32[256,2,1664]{2,0,1:T(8,128)}), f32[256,2,1664]{2,0,1:T(8,128)}) %all-reduce.5.cloned.1.call-update) | async-done | bytes 3407888 | tf_op jit(solution)/shard_map/psum | solution.py:54
  356.6 0.0 copy-done
  356.6 2.6 bitcast_add_fusion
  359.2 0.9 fusion.17
  360.0 0.0 copy-start.2
  360.1 1.0 copy-done.2
  361.0 5.9 %fusion.9 = f32[256,1024]{1,0:T(8,128)} fusion(bf16[2,1,1024,1664]{3,2,1,0:T(8,128)(2,1)} %all-to-all-done, bf16[256,1,1664]{2,0,1:T(8,128)(2,1)S(1)} %get-tuple-element.11, bf16[256,1,1664]{2,0,1:T(8,128)(2,1)S(1)} %get-tuple-element.10), kind=kOutput, calls=%fused_computation.18 | convolution fusion | flops 1745682432 | bytes 9568256 | tf_op jit(solution)/shard_map/tkf,kdf->td/dot_general | solution.py:61
  366.9 0.0 reduce-scatter.2.cloned.1.call-update
  366.9 0.0 copy-start.3
  366.9 0.0 all-gather.2.cloned.1.call-start
  367.0 60.1 %reduce-scatter.2.cloned.1.call-done = f32[16,1024]{1,0:T(8,128)} async-done(((f32[256,1024]{1,0:T(8,128)}), f32[16,1024]{1,0:T(8,128)}) %reduce-scatter.2.cloned.1.call-update) | async-done | bytes 65552 | tf_op jit(solution)/shard_map/reduce_scatter | solution.py:60
  427.1 0.0 all-gather.2.cloned.1.call-update
  427.1 0.0 all-reduce.7.cloned.1.call-start
  427.2 1.7 convolution_bitcast_fusion.1
  428.9 46.8 %psum.75 = bf16[256,2,16]{0,2,1:T(8,128)(2,1)S(1)} all-reduce(f32[256,2,16]{0,2,1:T(8,128)S(1)} %convolution_bitcast_fusion.1), channel_id=1, replica_groups=mesh['dp'=2,'ffn'=16,'hid'=16] {'ffn'}, use_global_device_ids=true, to_apply=%region_9.0 | all-reduce | flops 8192 | bytes 49152 | tf_op jit(solution)/shard_map/psum | solution.py:70
  475.7 0.0 copy-done.3
  475.7 1.1 convolution_multiply_fusion
  476.7 0.9 fusion.14
  477.6 0.0 all-reduce.7.cloned.1.call-update
  477.6 0.0 all-gather.2.cloned.1.call-done
  477.7 1.7 multiply_reduce_fusion.1
  479.4 27.5 %psum.76 = f32[256]{0:T(256)S(1)} all-reduce(f32[256]{0:T(256)S(1)} %get-tuple-element.12), channel_id=1, replica_groups=mesh['dp'=2,'ffn'=16,'hid'=16] {'hid'}, use_global_device_ids=true, to_apply=%region_11.0 | all-reduce | flops 256 | bytes 2048 | tf_op jit(solution)/shard_map/psum | solution.py:76
  506.9 1.2 multiply_reduce_fusion
  508.1 5.9 %psum.77 = f32[1024]{0:T(1024)} all-reduce(f32[1024]{0:T(1024)S(1)} %get-tuple-element.8), channel_id=1, replica_groups=mesh['dp'=2,'ffn'=16,'hid'=16] {'dp'}, use_global_device_ids=true, to_apply=%region_13.0 | all-reduce | flops 1024 | bytes 8192 | tf_op jit(solution)/shard_map/psum | solution.py:91
  513.9 11.1 %all-reduce.7.cloned.1.call-done = (f32[2,1024,16]{1,2,0:T(8,128)}, f32[2,16,1664]{2,1,0:T(8,128)}) async-done(((f32[2,1024,16]{1,2,0:T(8,128)}, f32[2,16,1664]{2,1,0:T(8,128)}), (f32[2,1024,16]{1,2,0:T(8,128)}, f32[2,16,1664]{2,1,0:T(8,128)})) %all-reduce.7.cloned.1.call-update) | async-done | bytes 344080 | tf_op jit(solution)/shard_map/psum | solution.py:91
  525.1 1.6 copy.15
  526.6 1.6 copy.16
  (3 shorter events, 0.0 us)
Async XLA Ops:
  7.2 349.4 %copy-start = (bf16[2,16,1664]{2,1,0:T(8,128)(2,1)S(1)}, bf16[2,16,1664]{2,1,0:T(8,128)(2,1)}, u32[]{:S(2)}) copy-start(bf16[2,16,1664]{2,1,0:T(8,128)(2,1)} %param.14) | copy-start | bytes 319492
  13.7 6.7 %copy-start.5 = (f32[1024]{0:T(1024)S(1)}, f32[1024]{0:T(1024)}, u32[]{:S(2)}) copy-start(f32[1024]{0:T(1024)} %param.9) | copy-start | bytes 12292
  13.7 7.3 %copy-start.1 = (bf16[256,1024]{1,0:T(8,128)(2,1)S(1)}, bf16[256,1024]{1,0:T(8,128)(2,1)}, u32[]{:S(2)}) copy-start(bf16[256,1024]{1,0:T(8,128)(2,1)} %param.8) | copy-start | bytes 1572868
  13.7 104.7 %copy-start.8 = (f32[256]{0:T(256)S(1)}, f32[256]{0:T(256)}, u32[]{:S(2)}) copy-start(f32[256]{0:T(256)} %param.10) | copy-start | bytes 3076
  13.7 128.7 %copy-start.7 = (f32[1024]{0:T(1024)S(1)}, f32[1024]{0:T(1024)}, u32[]{:S(2)}) copy-start(f32[1024]{0:T(1024)} %param.11) | copy-start | bytes 12292
  13.8 129.0 %all-to-all-start = ((bf16[2,1,1024,1664]{3,2,1,0:T(8,128)(2,1)}), bf16[2,1,1024,1664]{3,2,1,0:T(8,128)(2,1)}, u32[]{:S(2)}, u32[]{:S(2)}) async-start(bf16[2,1,1024,1664]{3,2,1,0:T(8,128)(2,1)} %pad_maximum_fusion), calls=%async_computation | async-start | bytes 13631488 | tf_op jit(solution)/shard_map/all_to_all | solution.py:50
  20.3 336.2 %all-reduce.5.cloned.1.call-start = ((), (), s32[]{:S(2)}) async-start(), calls=%async_computation.2 | async-start | bytes 6815744 | tf_op jit(solution)/shard_map/psum | solution.py:54
  149.4 0.8 copy-start.4
  149.4 50.3 %copy-start.6 = (bf16[16,1664]{1,0:T(8,128)(2,1)S(1)}, bf16[16,1664]{1,0:T(8,128)(2,1)}, u32[]{:S(2)}) copy-start(bf16[16,1664]{1,0:T(8,128)(2,1)} %param.15) | copy-start | bytes 159748
  149.5 277.6 %reduce-scatter.2.cloned.1.call-start = ((), (), s32[]{:S(2)}) async-start(), calls=%async_computation.3 | async-start | bytes 1114112 | tf_op jit(solution)/shard_map/reduce_scatter | solution.py:60
  360.0 1.0 copy-start.2
  366.9 108.8 %copy-start.3 = (bf16[256,1,1664]{2,0,1:T(8,128)(2,1)S(1)}, bf16[256,1,1664]{2,0,1:T(8,128)(2,1)}, u32[]{:S(2)}) copy-start(bf16[256,1,1664]{2,0,1:T(8,128)(2,1)} %copy-done.2) | copy-start | bytes 2555908
  366.9 110.7 %all-gather.2.cloned.1.call-start = ((), (), s32[]{:S(2)}) async-start(), calls=%async_computation.4 | async-start | bytes 1114112 | tf_op jit(solution)/shard_map/all_gather | solution.py:66
  427.1 97.9 %all-reduce.7.cloned.1.call-start = ((), (), s32[]{:S(2)}) async-start(), calls=%async_computation.5 | async-start | bytes 688128 | tf_op jit(solution)/shard_map/psum | solution.py:91
Sparse Core Ops, SparseCore 0:
  149.6 206.9 all-reduce.4
  367.0 60.0 reduce-scatter.1
  429.2 43.1 all-gather.1
  477.7 47.2 all-reduce.6
